TPU v7x, 256 devices: a whole 4x4x8 slice. The times are simulated.
256 devices in a mesh: rows: 64 (over x_lo, y, z), heads: 4 (over x_hi, core).
Axes of the slice: x: 4 (x_hi: 2, x_lo: 2; x = x_hi * 2 + x_lo), y: 4, z: 8, core: 2. Of those that a mesh axis runs over, the one named last changes fastest.
Arguments:
- new_qkv: bfloat16 [3, 49152, 5120], P(None, 'rows', 'heads'), may hold values from -1000 to 1000
- cache_kv: bfloat16 [2, 65536, 5120], P(None, 'rows', 'heads'), may hold values from -6 to 6
- q_gain: float32 [5120], P('heads'), may hold values from 0.5 to 1.5
- k_gain: float32 [5120], P('heads'), may hold values from 0.5 to 1.5
- new_list: int32 [384, 3], P('rows'), may hold values from 0 to 383, as said below
- new_count: int32 [384], P('rows'), may hold values from 1 to 3
- cache_list: int32 [384, 5], P('rows'), may hold values from 0 to 511, as said below
- cache_count: int32 [384], P('rows'), may hold values from 1 to 5
Outputs:
- attended: bfloat16 [49152, 5120], P('rows', 'heads')
Inputs may be any that keep to these rules, and one draw needn't show every extreme that they name: `new_list`: entry 0 of row t is t itself; the next new_count[t] - 1 entries are distinct tiles among t - 1 and t + 1; later entries repeat t. The first and the last query tile of each row shard list both adjacent tiles where they exist. `cache_list`: the live entries of row t are distinct cache tiles of the query tile's own row shard, or lie within 2 tiles beyond that shard's lower or upper edge; later entries repeat entry 0. The first and the last query tile of each row shard list min(5, available) tiles, the first one reaching below its shard where that exists, the last one above.
All inputs are finite; a program needn't handle non-finite values.
Results may differ from a plain program's by a relative error of at most 0.0085.
Values may be sent and summed in bfloat16 or wider, within the bound.
A program may use at most 128 MiB of HBM per device.

v0:
```python
import jax
import jax.numpy as jnp
from jax import lax
from jax.sharding import PartitionSpec as P

HEADS = 40
HEAD_DIM = 128
TILE = 128


def with_halo(block, sides, width):
    for axis, dim in sides:
        count = lax.axis_size(axis)
        forward = [(i, i + 1) for i in range(count - 1)]
        backward = [(target, source) for source, target in forward]
        low = lax.ppermute(
            lax.slice_in_dim(block, block.shape[dim] - width, None, axis=dim), axis, forward
        )
        high = lax.ppermute(lax.slice_in_dim(block, 0, width, axis=dim), axis, backward)
        block = jnp.concatenate([low, block, high], axis=dim)
    return block


def shifted(x, axis, by):
    count = lax.axis_size(axis)
    pairs = [(i, i + by) for i in range(count) if 0 <= i + by < count]
    return lax.ppermute(x, axis, pairs)


def on_device(new_qkv, cache_kv, q_gain, k_gain, new_list, new_count, cache_list, cache_count):
    groups = lax.axis_size("heads")
    rows_here = new_qkv.shape[1]
    group_width = new_qkv.shape[2]
    full_width = group_width * groups
    heads_here = HEADS // groups
    tiles_here = rows_here // TILE
    cache_tiles = cache_kv.shape[1] // TILE
    q_wide = new_qkv[0].astype(jnp.float32)
    k_wide = new_qkv[1].astype(jnp.float32)
    q_square, k_square = lax.psum(
        (jnp.sum(q_wide * q_wide, axis=1), jnp.sum(k_wide * k_wide, axis=1)), "heads"
    )
    q_normed = (q_wide * lax.rsqrt(q_square[:, None] / full_width + 1e-06) * q_gain).astype(
        jnp.bfloat16
    )
    k_normed = (k_wide * lax.rsqrt(k_square[:, None] / full_width + 1e-06) * k_gain).astype(
        jnp.bfloat16
    )
    local_pairs = jnp.stack([k_normed, new_qkv[2]])
    fresh_ext = with_halo(local_pairs, (("rows", 1),), TILE)
    shard_index = lax.axis_index("rows")
    from_below = shifted(cache_kv, "rows", 1)
    from_above = shifted(cache_kv, "rows", -1)
    cache_ext = jnp.concatenate([from_below, cache_kv, from_above], axis=1)
    cache_first = (shard_index - 1) * cache_tiles
    fresh_first = shard_index * tiles_here - 1
    fresh_blocks = fresh_ext.reshape(2, tiles_here + 2, TILE, group_width)
    cache_blocks = cache_ext.reshape(2, -1, TILE, group_width)
    fresh_slot = new_list - fresh_first
    cache_slot = cache_list - cache_first
    near_live = jnp.repeat(
        jnp.arange(new_list.shape[1], dtype=jnp.int32)[None, :] < new_count[:, None], TILE, axis=1
    )
    far_live = jnp.repeat(
        jnp.arange(cache_list.shape[1], dtype=jnp.int32)[None, :] < cache_count[:, None],
        TILE,
        axis=1,
    )
    live_keys = jnp.concatenate([near_live, far_live], axis=1)
    queries = q_normed.reshape(tiles_here, TILE, group_width)
    score_scale = HEAD_DIM ** (-0.5)

    def one_head(head_index, attended):
        start = head_index * HEAD_DIM
        query_head = lax.dynamic_slice_in_dim(queries, start, HEAD_DIM, 2)
        fresh_head = lax.dynamic_slice_in_dim(fresh_blocks, start, HEAD_DIM, 3)
        cache_head = lax.dynamic_slice_in_dim(cache_blocks, start, HEAD_DIM, 3)
        near_tiles = fresh_head[:, fresh_slot]
        far_tiles = cache_head[:, cache_slot]
        keys_vals = jnp.concatenate([near_tiles, far_tiles], axis=2).reshape(
            2, tiles_here, -1, HEAD_DIM
        )
        scores = (
            jnp.einsum("tqd,tkd->tqk", query_head, keys_vals[0], preferred_element_type=jnp.float32)
            * score_scale
        )
        scores = jnp.where(live_keys[:, None, :], scores, -jnp.inf)
        row_max = jnp.max(scores, axis=2, keepdims=True)
        weights = jnp.exp(scores - row_max)
        row_total = jnp.sum(weights, axis=2, keepdims=True)
        weights_bf = (weights / row_total).astype(jnp.bfloat16)
        mixed = jnp.einsum(
            "tqk,tkd->tqd", weights_bf, keys_vals[1], preferred_element_type=jnp.float32
        )
        mixed = mixed.astype(jnp.bfloat16).reshape(rows_here, HEAD_DIM)
        return lax.dynamic_update_slice_in_dim(attended, mixed, start, 1)

    empty = jnp.zeros((rows_here, group_width), jnp.bfloat16)
    return lax.fori_loop(0, heads_here, one_head, empty)


def solution(mesh):
    placed = (
        P(None, "rows", "heads"),
        P(None, "rows", "heads"),
        P("heads"),
        P("heads"),
        P("rows", None),
        P("rows"),
        P("rows", None),
        P("rows"),
    )
    return jax.shard_map(
        on_device, mesh=mesh, in_specs=placed, out_specs=P("rows", "heads"), check_vma=False
    )
```

profile of v0, /device:TPU:10, one launch (start us, length us, event | category | flops | bytes accessed | tf_op | source)
XLA Modules:
  0.0 321.3 jit_solution(1244664491008281092)
XLA Ops:
  0.0 3.9 %collective-permute-start.2 = (bf16[2,1024,1280]{2,1,0:T(8,128)(2,1)}, bf16[2,1024,1280]{2,1,0:T(8,128)(2,1)}, u32[]{:S(2)}, u32[]{:S(2)}) collective-permute-start(bf16[2,1024,1280]{2,1,0:T(8,128)(2,1)} %param.11), channel_id=1, source_target_pairs={{0,4},{4,8},{8,12},{12,16},{16,20},{20,24},{24,28},{28,32},{32,36}... | collective-permute-start | bytes 15728648 | tf_op jit(solution)/shard_map/ppermute | solution.py:27
  4.0 5.7 %collective-permute-start.3 = (bf16[2,1024,1280]{2,1,0:T(8,128)(2,1)}, bf16[2,1024,1280]{2,1,0:T(8,128)(2,1)}, u32[]{:S(2)}, u32[]{:S(2)}) collective-permute-start(bf16[2,1024,1280]{2,1,0:T(8,128)(2,1)} %param.11), channel_id=1, source_target_pairs={{4,0},{8,4},{12,8},{16,12},{20,16},{24,20},{28,24},{32,28},{36,32}... | collective-permute-start | bytes 15728648 | tf_op jit(solution)/shard_map/ppermute | solution.py:27
  9.7 3.0 fusion.13
  12.7 9.0 %all-reduce = (f32[768]{0:T(1024)S(1)}, f32[768]{0:T(1024)S(1)}) all-reduce(f32[768]{0:T(1024)S(1)} %get-tuple-element.146, f32[768]{0:T(1024)S(1)} %get-tuple-element.145), channel_id=1, replica_groups=mesh['rows'=64,'heads'=4] {'heads'}, use_global_device_ids=true, to_apply=%region_1.0 | all-reduce | flops 1536 | bytes 12288 | tf_op jit(solution)/shard_map/psum | solution.py:40
  21.7 2.1 fusion.15
  23.8 5.1 %fusion.17 = (bf16[1,768,1280]{2,1,0:T(8,128)(2,1)S(1)}, f32[1,768,1280]{2,1,0:T(8,128)}) fusion(bf16[3,768,1280]{2,1,0:T(8,128)(2,1)} %param.10), kind=kLoop, calls=%fused_computation.53 | loop fusion | flops 983040 | bytes 9830400 | tf_op jit(solution)/shard_map/slice | solution.py:49
  28.9 1.1 pad_maximum_fusion.4
  30.0 1.9 collective-permute-start
  32.0 126.8 %collective-permute-start.1 = (bf16[2,128,1280]{2,1,0:T(8,128)(2,1)}, bf16[2,128,1280]{2,1,0:T(8,128)(2,1)S(1)}, u32[]{:S(2)}, u32[]{:S(2)}) collective-permute-start(bf16[2,128,1280]{2,1,0:T(8,128)(2,1)} %get-tuple-element.172), channel_id=1, source_target_pairs={{4,0},{8,4},{12,8},{16,12},{20,16},{24,20},{28,24},{32,28},{36,32}... | collective-permute-start | bytes 1966088 | tf_op jit(solution)/shard_map/ppermute | solution.py:19
  159.7 3.9 %multiply_convert_fusion = bf16[6,128,1280]{2,1,0:T(8,128)(2,1)} fusion(f32[6,128,1280]{2,1,0:T(8,128)} %bitcast.62, f32[1280]{0:T(1024)S(1)} %copy-done.4, f32[6,128]{1,0:T(8,128)S(1)} %rsqrt_bitcast_fusion), kind=kLoop, calls=%fused_computation.37 | loop fusion | flops 2949120 | bytes 5906432 | tf_op jit(solution)/shard_map/convert_element_type | solution.py:43
  163.7 7.3 %collective-permute-done = bf16[2,128,1280]{2,1,0:T(8,128)(2,1)S(1)} collective-permute-done((bf16[2,128,1280]{2,1,0:T(8,128)(2,1)}, bf16[2,128,1280]{2,1,0:T(8,128)(2,1)S(1)}, u32[]{:S(2)}, u32[]{:S(2)}) %collective-permute-start) | collective-permute-done | bytes 655392 | tf_op jit(solution)/shard_map/ppermute | solution.py:16
  171.0 1.3 collective-permute-done.1
  172.3 5.7 %pad_maximum_fusion.2 = bf16[2,1024,1280]{2,1,0:T(8,128)(2,1)} fusion(bf16[2,128,1280]{2,1,0:T(8,128)(2,1)S(1)} %collective-permute-done.1, bf16[1,768,1280]{2,1,0:T(8,128)(2,1)S(1)} %get-tuple-element.169, bf16[1,768,1280]{2,1,0:T(8,128)(2,1)S(1)} %copy-done.2, bf16[2,128,1280]{2,1,0:T(8,128)(2,1)S(1)} %collective-permute-done), kind=kLoop, calls=%fused_computation.31 | loop fusion | flops 20971520 | bytes 10485760 | tf_op jit(solution)/shard_map/concatenate | solution.py:20
  178.1 25.1 %pad_maximum_fusion.1 = bf16[2,3072,1280]{2,1,0:T(8,128)(2,1)} fusion(bf16[2,1024,1280]{2,1,0:T(8,128)(2,1)} %collective-permute-done.3, bf16[2,1024,1280]{2,1,0:T(8,128)(2,1)S(1)} %bitcast.65, bf16[2,1024,1280]{2,1,0:T(8,128)(2,1)} %collective-permute-done.2), kind=kLoop, calls=%fused_computation.30 | loop fusion | flops 47185920 | bytes 31457280 | tf_op jit(solution)/shard_map/concatenate | solution.py:54
  203.2 1.4 broadcast_in_dim.56
  204.6 116.7 %while.13 = (s32[]{:T(128)}, bf16[768,1280]{1,0:T(8,128)(2,1)}, pred[6,1024]{1,0:T(8,128)(4,1)}, bf16[6,128,1280]{2,1,0:T(8,128)(2,1)}, bf16[2,8,128,1280]{3,2,1...) while((s32[]{:T(128)}, bf16[768,1280]{1,0:T(8,128)(2,1)}, ...), condition=%wide.region_7.8_spmd, body=%wide.region_4.7_spmd.sunk | while | flops 410619008 | bytes 44348924 | solution.py:99
  206.8 1.1 copy.26
  207.9 1.5 constant_dynamic-slice_fusion.5
  210.4 1.1 copy-done
  211.9 1.5 fusion.31
  213.4 1.6 fusion.32
  218.4 1.1 copy.26
  219.5 1.5 constant_dynamic-slice_fusion.5
  222.1 1.1 copy-done
  223.5 1.5 fusion.31
  225.0 1.6 fusion.32
  230.1 1.1 copy.26
  231.2 1.5 constant_dynamic-slice_fusion.5
  233.8 1.1 copy-done
  235.2 1.5 fusion.31
  236.7 1.6 fusion.32
  241.8 1.1 copy.26
  242.9 1.5 constant_dynamic-slice_fusion.5
  245.4 1.1 copy-done
  246.9 1.5 fusion.31
  248.4 1.6 fusion.32
  253.4 1.1 copy.26
  254.5 1.5 constant_dynamic-slice_fusion.5
  257.1 1.1 copy-done
  258.5 1.5 fusion.31
  260.0 1.6 fusion.32
  265.1 1.1 copy.26
  266.2 1.5 constant_dynamic-slice_fusion.5
  268.8 1.1 copy-done
  270.2 1.5 fusion.31
  271.7 1.6 fusion.32
  276.8 1.1 copy.26
  277.9 1.5 constant_dynamic-slice_fusion.5
  280.5 1.1 copy-done
  281.9 1.5 fusion.31
  283.4 1.6 fusion.32
  288.4 1.1 copy.26
  289.5 1.5 constant_dynamic-slice_fusion.5
  292.1 1.1 copy-done
  293.5 1.5 fusion.31
  295.0 1.6 fusion.32
  301.2 1.5 constant_dynamic-slice_fusion.5
  303.8 1.1 copy-done
  305.2 1.5 fusion.31
  306.7 1.6 fusion.32
  312.9 1.5 constant_dynamic-slice_fusion.5
  315.5 1.1 copy-done
  316.9 1.5 fusion.31
  318.4 1.6 fusion.32
  (205 shorter events, 51.1 us)
Async XLA Ops:
  0.0 21.7 %copy-start.3 = (f32[1280]{0:T(1024)S(1)}, f32[1280]{0:T(1024)}, u32[]{:S(2)}) copy-start(f32[1280]{0:T(1024)} %param.13) | copy-start | bytes 15364
  0.0 178.0 %collective-permute-start.2 = (bf16[2,1024,1280]{2,1,0:T(8,128)(2,1)}, bf16[2,1024,1280]{2,1,0:T(8,128)(2,1)}, u32[]{:S(2)}, u32[]{:S(2)}) collective-permute-start(bf16[2,1024,1280]{2,1,0:T(8,128)(2,1)} %param.11), channel_id=1, source_target_pairs={{0,4},{4,8},{8,12},{12,16},{16,20},{20,24},{24,28},{28,32},{32,36}... | collective-permute-start | bytes 15728648 | tf_op jit(solution)/shard_map/ppermute | solution.py:27
  4.0 174.1 %collective-permute-start.3 = (bf16[2,1024,1280]{2,1,0:T(8,128)(2,1)}, bf16[2,1024,1280]{2,1,0:T(8,128)(2,1)}, u32[]{:S(2)}, u32[]{:S(2)}) collective-permute-start(bf16[2,1024,1280]{2,1,0:T(8,128)(2,1)} %param.11), channel_id=1, source_target_pairs={{4,0},{8,4},{12,8},{16,12},{20,16},{24,20},{28,24},{32,28},{36,32}... | collective-permute-start | bytes 15728648 | tf_op jit(solution)/shard_map/ppermute | solution.py:27
  23.7 5.2 %copy-start.1 = (bf16[1,768,1280]{2,1,0:T(8,128)(2,1)}, bf16[1,768,1280]{2,1,0:T(8,128)(2,1)S(1)}, u32[]{:S(2)}) copy-start(bf16[1,768,1280]{2,1,0:T(8,128)(2,1)S(1)} %fusion.15) | copy-start | bytes 5898244
  28.9 129.9 %copy-start.8 = (s32[6]{0:T(128)S(1)}, s32[6]{0:T(128)}, u32[]{:S(2)}) copy-start(s32[6]{0:T(128)} %param.15) | copy-start | bytes 76
  28.9 130.1 %copy-start.9 = (s32[6]{0:T(128)S(1)}, s32[6]{0:T(128)}, u32[]{:S(2)}) copy-start(s32[6]{0:T(128)} %param.17) | copy-start | bytes 76
  28.9 130.8 %copy-start.7 = (s32[6,3]{0,1:T(4,128)S(1)}, s32[6,3]{0,1:T(4,128)}, u32[]{:S(2)}) copy-start(s32[6,3]{0,1:T(4,128)} %param.14) | copy-start | bytes 220
  28.9 130.8 %copy-start.6 = (s32[6,5]{1,0:T(8,128)S(1)}, s32[6,5]{1,0:T(8,128)}, u32[]{:S(2)}) copy-start(s32[6,5]{1,0:T(8,128)} %param.16) | copy-start | bytes 364
  28.9 130.8 %copy-start.4 = (f32[1280]{0:T(1024)S(1)}, f32[1280]{0:T(1024)}, u32[]{:S(2)}) copy-start(f32[1280]{0:T(1024)} %param.12) | copy-start | bytes 15364
  30.0 141.0 %collective-permute-start = (bf16[2,128,1280]{2,1,0:T(8,128)(2,1)}, bf16[2,128,1280]{2,1,0:T(8,128)(2,1)S(1)}, u32[]{:S(2)}, u32[]{:S(2)}) collective-permute-start(bf16[2,128,1280]{2,1,0:T(8,128)(2,1)} %get-tuple-element.171), channel_id=1, source_target_pairs={{0,4},{4,8},{8,12},{12,16},{16,20},{20,24},{24,28},{28,32},{32,36}... | collective-permute-start | bytes 1966088 | tf_op jit(solution)/shard_map/ppermute | solution.py:16
  32.0 140.3 %collective-permute-start.1 = (bf16[2,128,1280]{2,1,0:T(8,128)(2,1)}, bf16[2,128,1280]{2,1,0:T(8,128)(2,1)S(1)}, u32[]{:S(2)}, u32[]{:S(2)}) collective-permute-start(bf16[2,128,1280]{2,1,0:T(8,128)(2,1)} %get-tuple-element.172), channel_id=1, source_target_pairs={{4,0},{8,4},{12,8},{16,12},{20,16},{24,20},{28,24},{32,28},{36,32}... | collective-permute-start | bytes 1966088 | tf_op jit(solution)/shard_map/ppermute | solution.py:19
  159.0 13.3 %copy-start.2 = (bf16[1,768,1280]{2,1,0:T(8,128)(2,1)S(1)}, bf16[1,768,1280]{2,1,0:T(8,128)(2,1)}, u32[]{:S(2)}) copy-start(bf16[1,768,1280]{2,1,0:T(8,128)(2,1)} %copy-done.1) | copy-start | bytes 5898244
  159.7 18.3 %slice-start = ((s8[5242880]{0:T(1024)(128)(4,1)}), s8[4194304]{0:T(1024)(128)(4,1)S(1)}, s32[]{:S(2)}) async-start(s8[5242880]{0:T(1024)(128)(4,1)} %bitcast.64), calls=%async_computation | async-start | bytes 8388608
  163.7 14.4 %slice-start.1 = ((s8[5242880]{0:T(1024)(128)(4,1)}), s8[1048576]{0:T(1024)(128)(4,1)S(1)}, s32[]{:S(2)}) async-start(s8[5242880]{0:T(1024)(128)(4,1)} %bitcast.64), calls=%async_computation.1 | async-start | bytes 2097152
  210.3 1.3 copy-start
  211.8 1.5 copy-start.5
  222.0 1.3 copy-start
  223.5 1.5 copy-start.5
  233.6 1.3 copy-start
  235.2 1.5 copy-start.5
  245.3 1.3 copy-start
  246.8 1.5 copy-start.5
  257.0 1.3 copy-start
  258.5 1.5 copy-start.5
  268.6 1.3 copy-start
  270.2 1.5 copy-start.5
  280.3 1.3 copy-start
  281.9 1.5 copy-start.5
  292.0 1.3 copy-start
  293.5 1.5 copy-start.5
  303.6 1.3 copy-start
  305.2 1.5 copy-start.5
  315.3 1.3 copy-start
  316.9 1.5 copy-start.5
where the time goes:
time: 323 us; the launch traced here: 321 us
  starting transfers between devices  138 us (43%)
  local copies, waits for them, and re-layouts  77.5 us (24%)
  other arithmetic  65.3 us (20%)
  matrix products  21.4 us (7%)
  blocking collectives  8.95 us (3%)
  waiting for transfers between devices  8.61 us (3%)
    ppermute x1, starting transfers between devices, with_halo(): lax.ppermute(lax.slice_in_dim(block, 0, width, axis=dim), axis, backward)  127 us
    concatenate x1, other arithmetic, on_device(): cache_ext = jnp.concatenate([from_below, cache_kv, from_above], axis=1)  25.1 us
    gather x20, local copies, waits for them, and re-layouts, one_head(): near_tiles = fresh_head[:, fresh_slot]  18.7 us
    sub x10, other arithmetic, one_head(): weights = jnp.exp(scores - row_max)  15.6 us
    dynamic_slice x10, local copies, waits for them, and re-layouts, one_head(): cache_head = lax.dynamic_slice_in_dim(cache_blocks, start, HEAD_DIM, 3)  15.1 us
    dot_general x10, matrix products, one_head(): jnp.einsum('tqd,tkd->tqk', query_head, keys_vals[0], preferred_element_ty...  15 us
    while x40, local copies, waits for them, and re-layouts  11.3 us
    dynamic_slice x10, local copies, waits for them, and re-layouts, one_head(): fresh_head = lax.dynamic_slice_in_dim(fresh_blocks, start, HEAD_DIM, 3)  10.8 us
  transfers between devices with their start and end apart: 4, of which 2 were waited for; matrix products, arithmetic and copies ran while one was open for 7% of the time, Pallas kernels for 0%

commit v1 on v0

v1 whole, which is shorter than its diff:
```python
import functools

import jax
import jax.numpy as jnp
from jax import lax
from jax.experimental import pallas as pl
from jax.experimental.pallas import tpu as pltpu
from jax.sharding import PartitionSpec as P

HEADS = 40
HEAD_DIM = 128
TILE = 128
REACH = 2
CHUNKS = (2, 2, 2, 2, 1, 1)
EARLY = 3
MESH = pl.DeviceIdType.MESH


def kernel(
    new_list, new_count, cache_list, cache_count, q_gain, k_gain, new_qkv, cache_tiles, out, *scratch
):
    n_chunks = len(CHUNKS)
    news, caches = scratch[:n_chunks], scratch[n_chunks : 2 * n_chunks]
    (raw, q_scale, k_scale, halo_scale, sums, peer_sums, rates, halo_rates, bias, mixed) = scratch[
        2 * n_chunks : 2 * n_chunks + 10
    ]
    (raw_sem, local_sem, far_send, far_recv, near_send, near_recv, sum_send, sum_recv,
     rate_send, rate_recv, out_sem) = scratch[2 * n_chunks + 10 :]
    row, group = lax.axis_index("rows"), lax.axis_index("heads")
    n_rows, n_groups = lax.axis_size("rows"), lax.axis_size("heads")
    above, below = lax.rem(row + 1, n_rows), lax.rem(row + n_rows - 1, n_rows)
    peers = [lax.rem(group + step, n_groups) for step in range(1, n_groups)]
    rows_here, width = new_qkv.shape[1:]
    cache_count_here = cache_tiles.shape[1]
    tiles = rows_here // TILE
    heads = width // HEAD_DIM
    place = [(chunk, at) for chunk, count in enumerate(CHUNKS) for at in range(count)]

    def columns(head):
        return pl.ds(head * HEAD_DIM, HEAD_DIM)

    def local(source, target, sem):
        copy = pltpu.make_async_copy(source, target, sem)
        copy.start()
        return copy

    def remote(source, target, send, recv, device):
        return pltpu.make_async_remote_copy(
            src_ref=source, dst_ref=target, send_sem=send, recv_sem=recv,
            device_id=device, device_id_type=MESH,
        )

    raw_copies = [
        local(
            new_qkv.at[pl.ds(0, 2), pl.ds(t * TILE, TILE)],
            raw.at[:, pl.ds(t * TILE, TILE)],
            raw_sem.at[t],
        )
        for t in range(tiles)
    ]

    barrier = pltpu.get_barrier_semaphore()
    for device in [(above, group), (below, group)] + [(row, peer) for peer in peers]:
        pl.semaphore_signal(barrier, inc=1, device_id=device, device_id_type=MESH)
    pl.semaphore_wait(barrier, n_groups + 1)

    far, near = [], []
    for head, (chunk, at) in enumerate(place):
        cols = columns(head)
        there, edge = caches[chunk].at[at], news[chunk].at[at]
        far.append(
            (
                remote(
                    cache_tiles.at[:, pl.ds(cache_count_here - REACH, REACH), :, cols],
                    there.at[:, pl.ds(0, REACH)],
                    far_send.at[head, 0], far_recv.at[head, 0], (above, group),
                ),
                remote(
                    cache_tiles.at[:, pl.ds(0, REACH), :, cols],
                    there.at[:, pl.ds(REACH + cache_count_here, REACH)],
                    far_send.at[head, 1], far_recv.at[head, 1], (below, group),
                ),
            )
        )
        near.append(
            (
                remote(
                    new_qkv.at[pl.ds(1, 2), pl.ds(rows_here - TILE, TILE), cols],
                    edge.at[:, pl.ds(0, TILE)],
                    near_send.at[head, 0], near_recv.at[head, 0], (above, group),
                ),
                remote(
                    new_qkv.at[pl.ds(1, 2), pl.ds(0, TILE), cols],
                    edge.at[:, pl.ds(TILE + rows_here, TILE)],
                    near_send.at[head, 1], near_recv.at[head, 1], (below, group),
                ),
            )
        )

    for head in range(EARLY):
        for copy in far[head]:
            copy.start()

    held = []
    for head, (chunk, at) in enumerate(place):
        cols = columns(head)
        held.append(
            (
                local(
                    cache_tiles.at[:, :, :, cols],
                    caches[chunk].at[at, :, pl.ds(REACH, cache_count_here)],
                    local_sem.at[head, 0],
                ),
                local(
                    new_qkv.at[2, :, cols],
                    news[chunk].at[at, 1, pl.ds(TILE, rows_here)],
                    local_sem.at[head, 1],
                ),
            )
        )

    sums[...] = jnp.zeros_like(sums)
    for t in range(tiles):
        raw_copies[t].wait()
        for which in range(2):
            total = jnp.zeros((TILE, HEAD_DIM), jnp.float32)
            for head in range(heads):
                wide = raw[which, pl.ds(t * TILE, TILE), columns(head)].astype(jnp.float32)
                total += wide * wide
            sums[pl.ds(8 * which + t, 1), :] = jnp.sum(total.T, axis=0, keepdims=True)
    sum_copies = [
        remote(sums, peer_sums.at[i], sum_send.at[i], sum_recv.at[i], (row, peer))
        for i, peer in enumerate(peers)
    ]
    for copy in sum_copies:
        copy.start()
    for copy in sum_copies:
        copy.wait_recv()
    square = sums[...]
    for i in range(len(peers)):
        square += peer_sums[i]
    rates[...] = lax.rsqrt(square / (width * n_groups) + 1e-06)
    rate_copies = [
        remote(
            rates.at[pl.ds(8, 8)], halo_rates.at[side], rate_send.at[side], rate_recv.at[side],
            (device, group),
        )
        for side, device in enumerate((above, below))
    ]
    for copy in rate_copies:
        copy.start()
    for head in range(EARLY):
        for copy in near[head]:
            copy.start()
    for head in range(EARLY, heads):
        for copy in far[head] + near[head]:
            copy.start()

    def spread(line):
        return jnp.broadcast_to(line, (TILE, TILE)).T

    for t in range(tiles):
        q_scale[t] = spread(rates[pl.ds(t, 1), :])
        k_scale[t] = spread(rates[pl.ds(8 + t, 1), :])

    dead = jnp.full((1, TILE), -jnp.inf, jnp.float32)
    lowest_new = row * tiles
    for t in range(tiles):
        live = {i: jnp.zeros((1, TILE), jnp.int32) for i in (0, 2)}
        count = jnp.full((1, TILE), new_count[t], jnp.int32)
        for j in range(1, new_list.shape[0]):
            tile = jnp.full((1, TILE), new_list[j, t], jnp.int32) - (lowest_new + t)
            for i in live:
                live[i] = jnp.where((tile == i - 1) & (count > j), 1, live[i])
        count = jnp.full((1, TILE), cache_count[t], jnp.int32)
        for j in range(1, cache_list.shape[1]):
            live[3 + j] = jnp.where(count > j, 1, 0)
        for i, line in live.items():
            bias[t, i : i + 1, :] = jnp.where(line > 0, jnp.float32(0), dead)

    lowest_cache = row * cache_count_here - REACH
    power = HEAD_DIM ** (-0.5) * 1.4426950408889634

    def attend(chunk, at, head, t):
        start = pl.multiple_of(t * TILE, TILE)
        cols = pl.ds(pl.multiple_of(head * HEAD_DIM, HEAD_DIM), HEAD_DIM)
        near_rows = pl.ds(start, 3 * TILE)
        query = raw[0, pl.ds(start, TILE), cols].astype(jnp.float32)
        query = (query * q_scale[t] * q_gain[cols]).astype(jnp.bfloat16)
        far_tiles = [
            jnp.clip(cache_list[t, j] - lowest_cache, 0, cache_count_here + 2 * REACH - 1)
            for j in range(cache_list.shape[1])
        ]
        keys = [news[chunk][at, 0, near_rows, :]] + [caches[chunk][at, 0, i] for i in far_tiles]
        values = [news[chunk][at, 1, near_rows, :]] + [caches[chunk][at, 1, i] for i in far_tiles]
        scores = lax.dot_general(
            query, jnp.concatenate(keys, axis=0), (((1,), (1,)), ((), ())),
            preferred_element_type=jnp.float32,
        )
        parts = []
        for i in range(3 + len(far_tiles)):
            part = scores[:, i * TILE : (i + 1) * TILE]
            parts.append(part if i in (1, 3) else part + bias[t, i : i + 1, :])
        top = functools.reduce(jnp.maximum, parts)
        top = jnp.max(top, axis=1, keepdims=True)
        weights = [jnp.exp2((part - top) * power) for part in parts]
        total = jnp.sum(functools.reduce(jnp.add, weights), axis=1, keepdims=True)
        weights = jnp.concatenate([w.astype(jnp.bfloat16) for w in weights], axis=1)
        result = jnp.dot(
            weights, jnp.concatenate(values, axis=0), preferred_element_type=jnp.float32
        )
        mixed[head, pl.ds(start, TILE), :] = (result / total).astype(jnp.bfloat16)

    def normed_keys(chunk, at, head, t, scale):
        cols = pl.ds(pl.multiple_of(head * HEAD_DIM, HEAD_DIM), HEAD_DIM)
        wide = raw[1, pl.ds(pl.multiple_of(t * TILE, TILE), TILE), cols].astype(jnp.float32)
        return (wide * scale * k_gain[cols]).astype(jnp.bfloat16)

    out_copies = []
    first = 0
    for chunk, count in enumerate(CHUNKS):
        for head in range(first, first + count):
            for copy in held[head]:
                copy.wait()
            for copy in far[head]:
                copy.wait_recv()

        @pl.loop(0, count)
        def inner(at):
            head = first + at

            @pl.loop(0, tiles)
            def norm(t):
                news[chunk][at, 0, pl.ds(pl.multiple_of((t + 1) * TILE, TILE), TILE), :] = (
                    normed_keys(chunk, at, head, t, k_scale[t])
                )

            @pl.loop(1, tiles - 1)
            def middle(t):
                attend(chunk, at, head, t)

        if chunk == 0:
            for copy in rate_copies:
                copy.wait_recv()
            halo_scale[0] = spread(halo_rates[0, pl.ds(tiles - 1, 1), :])
            halo_scale[1] = spread(halo_rates[1, pl.ds(0, 1), :])
        for head in range(first, first + count):
            for copy in near[head]:
                copy.wait_recv()

        @pl.loop(0, count)
        def edges(at):
            head = first + at
            cols = pl.ds(pl.multiple_of(head * HEAD_DIM, HEAD_DIM), HEAD_DIM)
            for side in range(2):
                where = pl.ds(side * (TILE + rows_here), TILE)
                wide = news[chunk][at, 0, where, :].astype(jnp.float32)
                news[chunk][at, 0, where, :] = (wide * halo_scale[side] * k_gain[cols]).astype(
                    jnp.bfloat16
                )

            @pl.loop(0, 2)
            def ends(side):
                attend(chunk, at, head, side * (tiles - 1))

        for head in range(first, first + count):
            out_copies.append(local(mixed.at[head], out.at[:, columns(head)], out_sem.at[head]))
        first += count

    for copy in out_copies:
        copy.wait()
    for copy in sum_copies + rate_copies:
        copy.wait_send()
    for pair in far + near:
        for copy in pair:
            copy.wait_send()


def on_device(new_qkv, cache_kv, q_gain, k_gain, new_list, new_count, cache_list, cache_count):
    rows_here, width = new_qkv.shape[1:]
    cache_rows = cache_kv.shape[1]
    tiles = rows_here // TILE
    heads = width // HEAD_DIM
    groups = lax.axis_size("heads")
    in_smem = pl.BlockSpec(memory_space=pltpu.SMEM)
    in_vmem = pl.BlockSpec(memory_space=pltpu.VMEM)
    anywhere = pl.BlockSpec(memory_space=pl.ANY)
    dma = pltpu.SemaphoreType.DMA
    keys_here = (tiles + 3 + cache_list.shape[1]) * TILE
    return pl.pallas_call(
        kernel,
        out_shape=jax.ShapeDtypeStruct((rows_here, width), jnp.bfloat16),
        in_specs=[in_smem] * 4 + [in_vmem] * 2 + [anywhere] * 2,
        out_specs=anywhere,
        scratch_shapes=[
            pltpu.VMEM((count, 2, rows_here + 2 * TILE, HEAD_DIM), jnp.bfloat16)
            for count in CHUNKS
        ]
        + [
            pltpu.VMEM((count, 2, cache_rows // TILE + 2 * REACH, TILE, HEAD_DIM), jnp.bfloat16)
            for count in CHUNKS
        ]
        + [
            pltpu.VMEM((2, rows_here, width), jnp.bfloat16),
            pltpu.VMEM((tiles, TILE, HEAD_DIM), jnp.float32),
            pltpu.VMEM((tiles, TILE, HEAD_DIM), jnp.float32),
            pltpu.VMEM((2, TILE, HEAD_DIM), jnp.float32),
            pltpu.VMEM((16, TILE), jnp.float32),
            pltpu.VMEM((groups - 1, 16, TILE), jnp.float32),
            pltpu.VMEM((16, TILE), jnp.float32),
            pltpu.VMEM((2, 8, TILE), jnp.float32),
            pltpu.VMEM((tiles, 3 + cache_list.shape[1], TILE), jnp.float32),
            pltpu.VMEM((heads, rows_here, HEAD_DIM), jnp.bfloat16),
            dma((tiles,)),
            dma((heads, 2)),
            dma((heads, 2)),
            dma((heads, 2)),
            dma((heads, 2)),
            dma((heads, 2)),
            dma((groups - 1,)),
            dma((groups - 1,)),
            dma((2,)),
            dma((2,)),
            dma((heads,)),
        ],
        compiler_params=pltpu.CompilerParams(
            collective_id=0, has_side_effects=True, vmem_limit_bytes=56 * 2**20
        ),
        cost_estimate=pl.CostEstimate(
            flops=4 * rows_here * keys_here * width,
            bytes_accessed=2 * (4 * rows_here + 2 * cache_rows) * width,
            transcendentals=rows_here * keys_here * heads,
        ),
    )(
        new_list.T,
        new_count,
        cache_list,
        cache_count,
        q_gain,
        k_gain,
        new_qkv,
        cache_kv.reshape(2, cache_rows // TILE, TILE, width),
    )


def solution(mesh):
    placed = (
        P(None, "rows", "heads"),
        P(None, "rows", "heads"),
        P("heads"),
        P("heads"),
        P("rows", None),
        P("rows"),
        P("rows", None),
        P("rows"),
    )
    return jax.shard_map(
        on_device, mesh=mesh, in_specs=placed, out_specs=P("rows", "heads"), check_vma=False
    )
```

time: 323 us -> 97 us (0.30)
  the two profiles are of different devices: /device:TPU:10 before, /device:TPU:56 now
where the time goes in v1:
time: 97 us; the launch traced here: 96.9 us
  Pallas kernels  93.9 us (97%)
  local copies, waits for them, and re-layouts  2.94 us (3%)
    pallas_call x1, Pallas kernels, on_device(): pl.pallas_call(kernel, out_shape=jax.ShapeDtypeStruct((rows_here, width),...  93.9 us
    unnamed x1, local copies, waits for them, and re-layouts  2.94 us

profile of v1, /device:TPU:56, one launch (start us, length us, event | category | flops | bytes accessed | tf_op | source)
XLA Modules:
  0.0 96.9 jit_solution(607918155696146933)
XLA Ops:
  0.0 93.9 %shard_map.82 = bf16[768,1280]{1,0:T(8,128)(2,1)} custom-call(s32[3,6]{1,0:T(4,128)} %bitcast.3, s32[6]{0:T(128)} %new_count.1, s32[6,5]{1,0:T(8,128)} %cache_list.1, s32[6]{0:T(128)} %cache_count.1, f32[1280]{0:T(1024)} %q_gain.1, f32[1280]{0:T(1024)} %k_gain.1, bf16[3,768,1280]{2,1,0:T(8,128)(2,1)} %new_qkv.1, bf16[2,8,128,1280]{3,2,1,0:T(8,128)(2,1)} %bitcast.2), custom_call_target="tpu_custom_call" | custom-call | flops 7046430720 | bytes 13107200 | tf_op jit(solution)/shard_map/pallas_call | solution.py:290
  93.9 2.9 %copy.10 = bf16[768,1280]{1,0:T(8,128)(2,1)} copy(bf16[768,1280]{1,0:T(8,128)(2,1)} %shard_map.82) | data formatting | bytes 3932160

commit v2 on v1

--- a/solution.py
+++ b/solution.py
@@ -34,6 +34,7 @@
     cache_count_here = cache_tiles.shape[1]
     tiles = rows_here // TILE
     heads = width // HEAD_DIM
+    bend = n_rows // 2
     place = [(chunk, at) for chunk, count in enumerate(CHUNKS) for at in range(count)]
 
     def columns(head):
@@ -62,44 +63,96 @@
     barrier = pltpu.get_barrier_semaphore()
     for device in [(above, group), (below, group)] + [(row, peer) for peer in peers]:
         pl.semaphore_signal(barrier, inc=1, device_id=device, device_id_type=MESH)
-    pl.semaphore_wait(barrier, n_groups + 1)
+    for ones, others in (((bend - 1, bend), (0, n_rows - 1)), ((0, n_rows - 1), (bend - 1, bend))):
+
+        @pl.when((row == ones[0]) | (row == ones[1]))
+        def greet():
+            for other in others:
+                pl.semaphore_signal(barrier, inc=1, device_id=(other, group), device_id_type=MESH)
+
+    ends = (row == 0) | (row == n_rows - 1) | (row == bend - 1) | (row == bend)
+    pl.semaphore_wait(barrier, jnp.where(ends, n_groups + 3, n_groups + 1))
 
     far, near = [], []
+
+    def exchange(head, top, bottom, low, high, send, recv):
+        over_last = head % 2 == 0
+        middle, at_middle = (high, (n_rows - 1, group)) if over_last else (low, (0, group))
+        side = int(over_last)
+        return (
+            remote(top, low, send.at[head, 0], recv.at[head, 0], (above, group)),
+            remote(bottom, high, send.at[head, 1], recv.at[head, 1], (below, group)),
+            remote(top, middle, send.at[head, 0], recv.at[head, side], at_middle),
+            remote(middle, low, send.at[head, 1 - side], recv.at[head, 0], (bend, group)),
+        )
+
     for head, (chunk, at) in enumerate(place):
         cols = columns(head)
         there, edge = caches[chunk].at[at], news[chunk].at[at]
         far.append(
-            (
-                remote(
-                    cache_tiles.at[:, pl.ds(cache_count_here - REACH, REACH), :, cols],
-                    there.at[:, pl.ds(0, REACH)],
-                    far_send.at[head, 0], far_recv.at[head, 0], (above, group),
-                ),
-                remote(
-                    cache_tiles.at[:, pl.ds(0, REACH), :, cols],
-                    there.at[:, pl.ds(REACH + cache_count_here, REACH)],
-                    far_send.at[head, 1], far_recv.at[head, 1], (below, group),
-                ),
+            exchange(
+                head,
+                cache_tiles.at[:, pl.ds(cache_count_here - REACH, REACH), :, cols],
+                cache_tiles.at[:, pl.ds(0, REACH), :, cols],
+                there.at[:, pl.ds(0, REACH)],
+                there.at[:, pl.ds(REACH + cache_count_here, REACH)],
+                far_send,
+                far_recv,
             )
         )
         near.append(
-            (
-                remote(
-                    new_qkv.at[pl.ds(1, 2), pl.ds(rows_here - TILE, TILE), cols],
-                    edge.at[:, pl.ds(0, TILE)],
-                    near_send.at[head, 0], near_recv.at[head, 0], (above, group),
-                ),
-                remote(
-                    new_qkv.at[pl.ds(1, 2), pl.ds(0, TILE), cols],
-                    edge.at[:, pl.ds(TILE + rows_here, TILE)],
-                    near_send.at[head, 1], near_recv.at[head, 1], (below, group),
-                ),
+            exchange(
+                head,
+                new_qkv.at[pl.ds(1, 2), pl.ds(rows_here - TILE, TILE), cols],
+                new_qkv.at[pl.ds(1, 2), pl.ds(0, TILE), cols],
+                edge.at[:, pl.ds(0, TILE)],
+                edge.at[:, pl.ds(TILE + rows_here, TILE)],
+                near_send,
+                near_recv,
             )
         )
 
+    def start(ways):
+        pl.when((row < n_rows - 1) & (row != bend - 1))(ways[0].start)
+        pl.when(row == bend - 1)(ways[2].start)
+        pl.when(row > 0)(ways[1].start)
+
+    def arrive(ways):
+        pl.when(row > 0)(ways[0].wait_recv)
+        pl.when(row < n_rows - 1)(ways[1].wait_recv)
+
+    def relay(pair):
+        if 2 * pair >= heads:
+            return
+
+        @pl.when(row == n_rows - 1)
+        def even():
+            for ways in (far[2 * pair], near[2 * pair]):
+                ways[1].wait_recv()
+                ways[3].start()
+
+        @pl.when(row == 0)
+        def odd():
+            for ways in (far[2 * pair + 1], near[2 * pair + 1]):
+                ways[0].wait_recv()
+                ways[3].start()
+
     for head in range(EARLY):
-        for copy in far[head]:
-            copy.start()
+        start(far[head])
+
+    def clear(head, line):
+        chunk, at = place[head]
+        news[chunk][at, :, pl.ds(line, TILE), :] = jnp.zeros((2, TILE, HEAD_DIM), jnp.bfloat16)
+
+    @pl.when(row == 0)
+    def none_below():
+        for head in range(0, heads, 2):
+            clear(head, 0)
+
+    @pl.when(row == n_rows - 1)
+    def none_above():
+        for head in range(1, heads, 2):
+            clear(head, TILE + rows_here)
 
     held = []
     for head, (chunk, at) in enumerate(place):
@@ -150,11 +203,10 @@
     for copy in rate_copies:
         copy.start()
     for head in range(EARLY):
-        for copy in near[head]:
-            copy.start()
+        start(near[head])
     for head in range(EARLY, heads):
-        for copy in far[head] + near[head]:
-            copy.start()
+        start(far[head])
+        start(near[head])
 
     def spread(line):
         return jnp.broadcast_to(line, (TILE, TILE)).T
@@ -182,7 +234,7 @@
     power = HEAD_DIM ** (-0.5) * 1.4426950408889634
 
     def attend(chunk, at, head, t):
-        start = pl.multiple_of(t * TILE, TILE)
+        start = t * TILE
         cols = pl.ds(pl.multiple_of(head * HEAD_DIM, HEAD_DIM), HEAD_DIM)
         near_rows = pl.ds(start, 3 * TILE)
         query = raw[0, pl.ds(start, TILE), cols].astype(jnp.float32)
@@ -211,10 +263,10 @@
         )
         mixed[head, pl.ds(start, TILE), :] = (result / total).astype(jnp.bfloat16)
 
-    def normed_keys(chunk, at, head, t, scale):
+    def normed_keys(head, t):
         cols = pl.ds(pl.multiple_of(head * HEAD_DIM, HEAD_DIM), HEAD_DIM)
-        wide = raw[1, pl.ds(pl.multiple_of(t * TILE, TILE), TILE), cols].astype(jnp.float32)
-        return (wide * scale * k_gain[cols]).astype(jnp.bfloat16)
+        wide = raw[1, pl.ds(t * TILE, TILE), cols].astype(jnp.float32)
+        return (wide * k_scale[t] * k_gain[cols]).astype(jnp.bfloat16)
 
     out_copies = []
     first = 0
@@ -222,21 +274,17 @@
         for head in range(first, first + count):
             for copy in held[head]:
                 copy.wait()
-            for copy in far[head]:
-                copy.wait_recv()
+            arrive(far[head])
+        relay(2 * chunk)
 
         @pl.loop(0, count)
         def inner(at):
             head = first + at
 
-            @pl.loop(0, tiles)
-            def norm(t):
-                news[chunk][at, 0, pl.ds(pl.multiple_of((t + 1) * TILE, TILE), TILE), :] = (
-                    normed_keys(chunk, at, head, t, k_scale[t])
-                )
-
-            @pl.loop(1, tiles - 1)
-            def middle(t):
+            for t in range(tiles):
+                news[chunk][at, 0, pl.ds((t + 1) * TILE, TILE), :] = normed_keys(head, t)
+
+            for t in range(1, tiles - 1):
                 attend(chunk, at, head, t)
 
         if chunk == 0:
@@ -245,23 +293,26 @@
             halo_scale[0] = spread(halo_rates[0, pl.ds(tiles - 1, 1), :])
             halo_scale[1] = spread(halo_rates[1, pl.ds(0, 1), :])
         for head in range(first, first + count):
-            for copy in near[head]:
-                copy.wait_recv()
+            arrive(near[head])
+        relay(2 * chunk + 1)
 
         @pl.loop(0, count)
         def edges(at):
             head = first + at
             cols = pl.ds(pl.multiple_of(head * HEAD_DIM, HEAD_DIM), HEAD_DIM)
-            for side in range(2):
+
+            def norm_halo(side):
                 where = pl.ds(side * (TILE + rows_here), TILE)
                 wide = news[chunk][at, 0, where, :].astype(jnp.float32)
                 news[chunk][at, 0, where, :] = (wide * halo_scale[side] * k_gain[cols]).astype(
                     jnp.bfloat16
                 )
 
-            @pl.loop(0, 2)
-            def ends(side):
-                attend(chunk, at, head, side * (tiles - 1))
+            pl.when(row > 0)(lambda: norm_halo(0))
+            pl.when(row < n_rows - 1)(lambda: norm_halo(1))
+
+            for t in (0, tiles - 1):
+                attend(chunk, at, head, t)
 
         for head in range(first, first + count):
             out_copies.append(local(mixed.at[head], out.at[:, columns(head)], out_sem.at[head]))
@@ -271,9 +322,14 @@
         copy.wait()
     for copy in sum_copies + rate_copies:
         copy.wait_send()
-    for pair in far + near:
-        for copy in pair:
-            copy.wait_send()
+    for head in range(heads):
+        for ways in (far[head], near[head]):
+            if head % 2 == 0:
+                ways[0].wait_send()
+                pl.when(row > 0)(ways[1].wait_send)
+            else:
+                pl.when(row < n_rows - 1)(ways[0].wait_send)
+                ways[1].wait_send()
 
 
 def on_device(new_qkv, cache_kv, q_gain, k_gain, new_list, new_count, cache_list, cache_count):

time: 97 us -> 60 us (0.62)
  the two profiles are of different devices: /device:TPU:56 before, /device:TPU:32 now
where the time goes in v2:
time: 60 us; the launch traced here: 59.6 us
  Pallas kernels  56.7 us (94%)
  local copies, waits for them, and re-layouts  2.94 us (5%)
    pallas_call x1, Pallas kernels, on_device(): pl.pallas_call(kernel, out_shape=jax.ShapeDtypeStruct((rows_here, width),...  56.7 us
    unnamed x1, local copies, waits for them, and re-layouts  2.94 us

profile of v2, /device:TPU:32, one launch (start us, length us, event | category | flops | bytes accessed | tf_op | source)
XLA Modules:
  0.0 59.6 jit_solution(6070630173038515463)
XLA Ops:
  0.0 56.7 %shard_map.82 = bf16[768,1280]{1,0:T(8,128)(2,1)} custom-call(s32[3,6]{1,0:T(4,128)} %bitcast.3, s32[6]{0:T(128)} %new_count.1, s32[6,5]{1,0:T(8,128)} %cache_list.1, s32[6]{0:T(128)} %cache_count.1, f32[1280]{0:T(1024)} %q_gain.1, f32[1280]{0:T(1024)} %k_gain.1, bf16[3,768,1280]{2,1,0:T(8,128)(2,1)} %new_qkv.1, bf16[2,8,128,1280]{3,2,1,0:T(8,128)(2,1)} %bitcast.2), custom_call_target="tpu_custom_call" | custom-call | flops 7046430720 | bytes 13107200 | tf_op jit(solution)/shard_map/pallas_call | solution.py:346
  56.7 2.9 %copy.10 = bf16[768,1280]{1,0:T(8,128)(2,1)} copy(bf16[768,1280]{1,0:T(8,128)(2,1)} %shard_map.82) | data formatting | bytes 3932160

commit v3 on v2

--- a/solution.py
+++ b/solution.py
@@ -21,11 +21,11 @@
 ):
     n_chunks = len(CHUNKS)
     news, caches = scratch[:n_chunks], scratch[n_chunks : 2 * n_chunks]
-    (raw, q_scale, k_scale, halo_scale, sums, peer_sums, rates, halo_rates, bias, mixed) = scratch[
-        2 * n_chunks : 2 * n_chunks + 10
+    (raw, q_scale, k_scale, halo_scale, sums, peer_sums, rates, halo_rates, bias) = scratch[
+        2 * n_chunks : 2 * n_chunks + 9
     ]
     (raw_sem, local_sem, far_send, far_recv, near_send, near_recv, sum_send, sum_recv,
-     rate_send, rate_recv, out_sem) = scratch[2 * n_chunks + 10 :]
+     rate_send, rate_recv) = scratch[2 * n_chunks + 9 :]
     row, group = lax.axis_index("rows"), lax.axis_index("heads")
     n_rows, n_groups = lax.axis_size("rows"), lax.axis_size("heads")
     above, below = lax.rem(row + 1, n_rows), lax.rem(row + n_rows - 1, n_rows)
@@ -261,14 +261,13 @@
         result = jnp.dot(
             weights, jnp.concatenate(values, axis=0), preferred_element_type=jnp.float32
         )
-        mixed[head, pl.ds(start, TILE), :] = (result / total).astype(jnp.bfloat16)
+        out[pl.ds(start, TILE), cols] = (result / total).astype(jnp.bfloat16)
 
     def normed_keys(head, t):
         cols = pl.ds(pl.multiple_of(head * HEAD_DIM, HEAD_DIM), HEAD_DIM)
         wide = raw[1, pl.ds(t * TILE, TILE), cols].astype(jnp.float32)
         return (wide * k_scale[t] * k_gain[cols]).astype(jnp.bfloat16)
 
-    out_copies = []
     first = 0
     for chunk, count in enumerate(CHUNKS):
         for head in range(first, first + count):
@@ -314,12 +313,8 @@
             for t in (0, tiles - 1):
                 attend(chunk, at, head, t)
 
-        for head in range(first, first + count):
-            out_copies.append(local(mixed.at[head], out.at[:, columns(head)], out_sem.at[head]))
         first += count
 
-    for copy in out_copies:
-        copy.wait()
     for copy in sum_copies + rate_copies:
         copy.wait_send()
     for head in range(heads):
@@ -345,9 +340,9 @@
     keys_here = (tiles + 3 + cache_list.shape[1]) * TILE
     return pl.pallas_call(
         kernel,
-        out_shape=jax.ShapeDtypeStruct((rows_here, width), jnp.bfloat16),
+        out_shape=pltpu.VMEM((rows_here, width), jnp.bfloat16),
         in_specs=[in_smem] * 4 + [in_vmem] * 2 + [anywhere] * 2,
-        out_specs=anywhere,
+        out_specs=in_vmem,
         scratch_shapes=[
             pltpu.VMEM((count, 2, rows_here + 2 * TILE, HEAD_DIM), jnp.bfloat16)
             for count in CHUNKS
@@ -366,7 +361,6 @@
             pltpu.VMEM((16, TILE), jnp.float32),
             pltpu.VMEM((2, 8, TILE), jnp.float32),
             pltpu.VMEM((tiles, 3 + cache_list.shape[1], TILE), jnp.float32),
-            pltpu.VMEM((heads, rows_here, HEAD_DIM), jnp.bfloat16),
             dma((tiles,)),
             dma((heads, 2)),
             dma((heads, 2)),
@@ -377,10 +371,9 @@
             dma((groups - 1,)),
             dma((2,)),
             dma((2,)),
-            dma((heads,)),
         ],
         compiler_params=pltpu.CompilerParams(
-            collective_id=0, has_side_effects=True, vmem_limit_bytes=56 * 2**20
+            collective_id=0, has_side_effects=True, vmem_limit_bytes=60 * 2**20
         ),
         cost_estimate=pl.CostEstimate(
             flops=4 * rows_here * keys_here * width,

time: 60 us -> 57.6 us (0.960)
  local copies, waits for them, and re-layouts: 2.94 us -> 1.27 us
  Pallas kernels: 56.7 us -> 55.9 us
    unnamed x1, local copies, waits for them, and re-layouts: 2.94 us -> 1.27 us
    pallas_call x1, Pallas kernels: 56.7 us -> 55.9 us  [on_device(): pl.pallas_call(kernel, out_shape=pltpu.VMEM((rows_here, width), jnp.bfloa...]
where the time goes in v3:
time: 57.6 us; the launch traced here: 57.1 us
  Pallas kernels  55.9 us (97%)
  local copies, waits for them, and re-layouts  1.27 us (2%)
    pallas_call x1, Pallas kernels, on_device(): pl.pallas_call(kernel, out_shape=pltpu.VMEM((rows_here, width), jnp.bfloa...  55.9 us
    unnamed x1, local copies, waits for them, and re-layouts  1.27 us

profile of v3, /device:TPU:32, one launch (start us, length us, event | category | flops | bytes accessed | tf_op | source)
XLA Modules:
  0.0 57.1 jit_solution(15771157235829893724)
XLA Ops:
  0.0 55.9 %shard_map.82 = bf16[768,1280]{1,0:T(8,128)(2,1)S(1)} custom-call(s32[3,6]{1,0:T(4,128)} %bitcast.3, s32[6]{0:T(128)} %new_count.1, s32[6,5]{1,0:T(8,128)} %cache_list.1, s32[6]{0:T(128)} %cache_count.1, f32[1280]{0:T(1024)} %q_gain.1, f32[1280]{0:T(1024)} %k_gain.1, bf16[3,768,1280]{2,1,0:T(8,128)(2,1)} %new_qkv.1, bf16[2,8,128,1280]{3,2,1,0:T(8,128)(2,1)} %bitcast.2), custom_call_target="tpu_custom_call" | custom-call | flops 7046430720 | bytes 13107200 | tf_op jit(solution)/shard_map/pallas_call | solution.py:341
  55.9 1.3 %copy.10 = bf16[768,1280]{1,0:T(8,128)(2,1)} copy(bf16[768,1280]{1,0:T(8,128)(2,1)S(1)} %shard_map.82) | data formatting | bytes 3932160

commit v4 on v3

--- a/solution.py
+++ b/solution.py
@@ -11,7 +11,8 @@
 HEAD_DIM = 128
 TILE = 128
 REACH = 2
-CHUNKS = (2, 2, 2, 2, 1, 1)
+CHUNKS = (2, 2, 2, 1, 1, 1, 1)
+LATE = 3
 EARLY = 3
 MESH = pl.DeviceIdType.MESH
 
@@ -112,10 +113,14 @@
             )
         )
 
-    def start(ways):
-        pl.when((row < n_rows - 1) & (row != bend - 1))(ways[0].start)
-        pl.when(row == bend - 1)(ways[2].start)
-        pl.when(row > 0)(ways[1].start)
+    def start(kind, head):
+        @pl.when(row == bend - 1)
+        def ahead():
+            for ways in kind[2 * head : 2 * head + 2]:
+                ways[2].start()
+
+        pl.when((row < n_rows - 1) & (row != bend - 1))(kind[head][0].start)
+        pl.when(row > 0)(kind[head][1].start)
 
     def arrive(ways):
         pl.when(row > 0)(ways[0].wait_recv)
@@ -138,7 +143,7 @@
                 ways[3].start()
 
     for head in range(EARLY):
-        start(far[head])
+        start(far, head)
 
     def clear(head, line):
         chunk, at = place[head]
@@ -203,10 +208,13 @@
     for copy in rate_copies:
         copy.start()
     for head in range(EARLY):
-        start(near[head])
-    for head in range(EARLY, heads):
-        start(far[head])
-        start(near[head])
+        start(near, head)
+    for head in range(EARLY, heads - LATE):
+        start(far, head)
+        start(near, head)
+    for kind in (far, near):
+        for head in range(heads - LATE, heads):
+            start(kind, head)
 
     def spread(line):
         return jnp.broadcast_to(line, (TILE, TILE)).T
@@ -233,10 +241,12 @@
     lowest_cache = row * cache_count_here - REACH
     power = HEAD_DIM ** (-0.5) * 1.4426950408889634
 
-    def attend(chunk, at, head, t):
+    def attend(chunk, at, head, t, without=None):
         start = t * TILE
         cols = pl.ds(pl.multiple_of(head * HEAD_DIM, HEAD_DIM), HEAD_DIM)
         near_rows = pl.ds(start, 3 * TILE)
+        if without is not None:
+            near_rows = pl.ds(start + (TILE if without == 0 else 0), 2 * TILE)
         query = raw[0, pl.ds(start, TILE), cols].astype(jnp.float32)
         query = (query * q_scale[t] * q_gain[cols]).astype(jnp.bfloat16)
         far_tiles = [
@@ -250,9 +260,9 @@
             preferred_element_type=jnp.float32,
         )
         parts = []
-        for i in range(3 + len(far_tiles)):
+        for i, column in enumerate(i for i in range(3 + len(far_tiles)) if i != without):
             part = scores[:, i * TILE : (i + 1) * TILE]
-            parts.append(part if i in (1, 3) else part + bias[t, i : i + 1, :])
+            parts.append(part if column in (1, 3) else part + bias[t, column : column + 1, :])
         top = functools.reduce(jnp.maximum, parts)
         top = jnp.max(top, axis=1, keepdims=True)
         weights = [jnp.exp2((part - top) * power) for part in parts]
@@ -261,15 +271,37 @@
         result = jnp.dot(
             weights, jnp.concatenate(values, axis=0), preferred_element_type=jnp.float32
         )
+        if without is not None:
+            return query, top, total, result
         out[pl.ds(start, TILE), cols] = (result / total).astype(jnp.bfloat16)
+
+    def finish(chunk, at, head, t, without, query, top, total, result):
+        cols = pl.ds(head * HEAD_DIM, HEAD_DIM)
+        halo = pl.ds((t + without) * TILE, TILE)
+        scores = lax.dot_general(
+            query, news[chunk][at, 0, halo, :], (((1,), (1,)), ((), ())),
+            preferred_element_type=jnp.float32,
+        )
+        scores += bias[t, without : without + 1, :]
+        peak = jnp.maximum(top, jnp.max(scores, axis=1, keepdims=True))
+        weights = jnp.exp2((scores - peak) * power)
+        fade = jnp.exp2((top - peak) * power)
+        total = total * fade + jnp.sum(weights, axis=1, keepdims=True)
+        result = result * fade + jnp.dot(
+            weights.astype(jnp.bfloat16), news[chunk][at, 1, halo, :],
+            preferred_element_type=jnp.float32,
+        )
+        out[pl.ds(t * TILE, TILE), cols] = (result / total).astype(jnp.bfloat16)
 
     def normed_keys(head, t):
         cols = pl.ds(pl.multiple_of(head * HEAD_DIM, HEAD_DIM), HEAD_DIM)
         wide = raw[1, pl.ds(t * TILE, TILE), cols].astype(jnp.float32)
         return (wide * k_scale[t] * k_gain[cols]).astype(jnp.bfloat16)
 
-    first = 0
-    for chunk, count in enumerate(CHUNKS):
+    firsts = [sum(CHUNKS[:chunk]) for chunk in range(n_chunks)]
+
+    def inner(chunk):
+        first, count = firsts[chunk], CHUNKS[chunk]
         for head in range(first, first + count):
             for copy in held[head]:
                 copy.wait()
@@ -277,15 +309,15 @@
         relay(2 * chunk)
 
         @pl.loop(0, count)
-        def inner(at):
+        def one(at):
             head = first + at
-
             for t in range(tiles):
                 news[chunk][at, 0, pl.ds((t + 1) * TILE, TILE), :] = normed_keys(head, t)
-
             for t in range(1, tiles - 1):
                 attend(chunk, at, head, t)
 
+    def outer(chunk):
+        first, count = firsts[chunk], CHUNKS[chunk]
         if chunk == 0:
             for copy in rate_copies:
                 copy.wait_recv()
@@ -296,24 +328,39 @@
         relay(2 * chunk + 1)
 
         @pl.loop(0, count)
-        def edges(at):
+        def one(at):
             head = first + at
-            cols = pl.ds(pl.multiple_of(head * HEAD_DIM, HEAD_DIM), HEAD_DIM)
-
-            def norm_halo(side):
-                where = pl.ds(side * (TILE + rows_here), TILE)
-                wide = news[chunk][at, 0, where, :].astype(jnp.float32)
-                news[chunk][at, 0, where, :] = (wide * halo_scale[side] * k_gain[cols]).astype(
-                    jnp.bfloat16
-                )
-
-            pl.when(row > 0)(lambda: norm_halo(0))
-            pl.when(row < n_rows - 1)(lambda: norm_halo(1))
-
+            norm_halos(chunk, at, head)
             for t in (0, tiles - 1):
                 attend(chunk, at, head, t)
 
-        first += count
+    def norm_halos(chunk, at, head):
+        cols = pl.ds(pl.multiple_of(head * HEAD_DIM, HEAD_DIM), HEAD_DIM)
+
+        def norm_halo(side):
+            where = pl.ds(side * (TILE + rows_here), TILE)
+            wide = news[chunk][at, 0, where, :].astype(jnp.float32)
+            news[chunk][at, 0, where, :] = (wide * halo_scale[side] * k_gain[cols]).astype(
+                jnp.bfloat16
+            )
+
+        pl.when(row > 0)(lambda: norm_halo(0))
+        pl.when(row < n_rows - 1)(lambda: norm_halo(1))
+
+    for chunk in range(n_chunks - LATE):
+        inner(chunk)
+        outer(chunk)
+    for chunk in range(n_chunks - LATE, n_chunks):
+        inner(chunk)
+    chunk, head = n_chunks - 1, heads - 1
+    sides = ((0, 0), (tiles - 1, 2))
+    begun = [attend(chunk, 0, head, t, without) for t, without in sides]
+    for before in range(n_chunks - LATE, n_chunks - 1):
+        outer(before)
+    arrive(near[head])
+    norm_halos(chunk, 0, head)
+    for (t, without), state in zip(sides, begun):
+        finish(chunk, 0, head, t, without, *state)
 
     for copy in sum_copies + rate_copies:
         copy.wait_send()

time: 57.6 us -> 56.9 us (0.988)
  no operation moved by 1% of the time
where the time goes in v4:
time: 56.9 us; the launch traced here: 56.7 us
  Pallas kernels  55.5 us (98%)
  local copies, waits for them, and re-layouts  1.27 us (2%)
    pallas_call x1, Pallas kernels, on_device(): pl.pallas_call(kernel, out_shape=pltpu.VMEM((rows_here, width), jnp.bfloa...  55.5 us
    unnamed x1, local copies, waits for them, and re-layouts  1.27 us

profile of v4, /device:TPU:32, one launch (start us, length us, event | category | flops | bytes accessed | tf_op | source)
XLA Modules:
  0.0 56.7 jit_solution(6869895975913024163)
XLA Ops:
  0.0 55.5 %shard_map.82 = bf16[768,1280]{1,0:T(8,128)(2,1)S(1)} custom-call(s32[3,6]{1,0:T(4,128)} %bitcast.3, s32[6]{0:T(128)} %new_count.1, s32[6,5]{1,0:T(8,128)} %cache_list.1, s32[6]{0:T(128)} %cache_count.1, f32[1280]{0:T(1024)} %q_gain.1, f32[1280]{0:T(1024)} %k_gain.1, bf16[3,768,1280]{2,1,0:T(8,128)(2,1)} %new_qkv.1, bf16[2,8,128,1280]{3,2,1,0:T(8,128)(2,1)} %bitcast.2), custom_call_target="tpu_custom_call" | custom-call | flops 7046430720 | bytes 13107200 | tf_op jit(solution)/shard_map/pallas_call | solution.py:388
  55.5 1.3 %copy.10 = bf16[768,1280]{1,0:T(8,128)(2,1)} copy(bf16[768,1280]{1,0:T(8,128)(2,1)S(1)} %shard_map.82) | data formatting | bytes 3932160

commit v5 on v4

--- a/solution.py
+++ b/solution.py
@@ -62,17 +62,21 @@
     ]
 
     barrier = pltpu.get_barrier_semaphore()
-    for device in [(above, group), (below, group)] + [(row, peer) for peer in peers]:
+    def greet(device):
         pl.semaphore_signal(barrier, inc=1, device_id=device, device_id_type=MESH)
-    for ones, others in (((bend - 1, bend), (0, n_rows - 1)), ((0, n_rows - 1), (bend - 1, bend))):
-
-        @pl.when((row == ones[0]) | (row == ones[1]))
-        def greet():
-            for other in others:
-                pl.semaphore_signal(barrier, inc=1, device_id=(other, group), device_id_type=MESH)
-
-    ends = (row == 0) | (row == n_rows - 1) | (row == bend - 1) | (row == bend)
-    pl.semaphore_wait(barrier, jnp.where(ends, n_groups + 3, n_groups + 1))
+
+    pl.when(row < n_rows - 1)(lambda: greet((above, group)))
+    pl.when(row > 0)(lambda: greet((below, group)))
+    for peer in peers:
+        greet((row, peer))
+    pl.when((row == 0) | (row == n_rows - 1))(lambda: greet((bend - 1, group)))
+
+    @pl.when(row == bend)
+    def greet_ends():
+        greet((0, group))
+        greet((n_rows - 1, group))
+
+    pl.semaphore_wait(barrier, jnp.where(row == bend - 1, n_groups + 3, n_groups + 1))
 
     far, near = [], []
 
@@ -205,8 +209,8 @@
         )
         for side, device in enumerate((above, below))
     ]
-    for copy in rate_copies:
-        copy.start()
+    pl.when(row < n_rows - 1)(rate_copies[0].start)
+    pl.when(row > 0)(rate_copies[1].start)
     for head in range(EARLY):
         start(near, head)
     for head in range(EARLY, heads - LATE):
@@ -319,8 +323,8 @@
     def outer(chunk):
         first, count = firsts[chunk], CHUNKS[chunk]
         if chunk == 0:
-            for copy in rate_copies:
-                copy.wait_recv()
+            pl.when(row > 0)(rate_copies[0].wait_recv)
+            pl.when(row < n_rows - 1)(rate_copies[1].wait_recv)
             halo_scale[0] = spread(halo_rates[0, pl.ds(tiles - 1, 1), :])
             halo_scale[1] = spread(halo_rates[1, pl.ds(0, 1), :])
         for head in range(first, first + count):
@@ -362,8 +366,10 @@
     for (t, without), state in zip(sides, begun):
         finish(chunk, 0, head, t, without, *state)
 
-    for copy in sum_copies + rate_copies:
+    for copy in sum_copies:
         copy.wait_send()
+    pl.when(row < n_rows - 1)(rate_copies[0].wait_send)
+    pl.when(row > 0)(rate_copies[1].wait_send)
     for head in range(heads):
         for ways in (far[head], near[head]):
             if head % 2 == 0:

time: 56.9 us -> 56.8 us (level)
  the two profiles are of different devices: /device:TPU:32 before, /device:TPU:6 now
where the time goes in v5:
time: 56.8 us; the launch traced here: 56.7 us
  Pallas kernels  55.4 us (98%)
  local copies, waits for them, and re-layouts  1.27 us (2%)
    pallas_call x1, Pallas kernels, on_device(): pl.pallas_call(kernel, out_shape=pltpu.VMEM((rows_here, width), jnp.bfloa...  55.4 us
    unnamed x1, local copies, waits for them, and re-layouts  1.27 us

profile of v5, /device:TPU:6, one launch (start us, length us, event | category | flops | bytes accessed | tf_op | source)
XLA Modules:
  0.0 56.7 jit_solution(13003693531777198848)
XLA Ops:
  0.0 55.4 %shard_map.82 = bf16[768,1280]{1,0:T(8,128)(2,1)S(1)} custom-call(s32[3,6]{1,0:T(4,128)} %bitcast.3, s32[6]{0:T(128)} %new_count.1, s32[6,5]{1,0:T(8,128)} %cache_list.1, s32[6]{0:T(128)} %cache_count.1, f32[1280]{0:T(1024)} %q_gain.1, f32[1280]{0:T(1024)} %k_gain.1, bf16[3,768,1280]{2,1,0:T(8,128)(2,1)} %new_qkv.1, bf16[2,8,128,1280]{3,2,1,0:T(8,128)(2,1)} %bitcast.2), custom_call_target="tpu_custom_call" | custom-call | flops 7046430720 | bytes 13107200 | tf_op jit(solution)/shard_map/pallas_call | solution.py:394
  55.4 1.3 %copy.10 = bf16[768,1280]{1,0:T(8,128)(2,1)} copy(bf16[768,1280]{1,0:T(8,128)(2,1)S(1)} %shard_map.82) | data formatting | bytes 3932160
